TPU v7x, 256 devices: a whole 4x4x8 slice. The times are simulated.
256 devices in a mesh: wide: 64 (over x_hi, z, y), narrow: 4 (over x_lo, core).
Axes of the slice: x: 4 (x_hi: 2, x_lo: 2; x = x_hi * 2 + x_lo), y: 4, z: 8, core: 2. Of those that a mesh axis runs over, the one named last changes fastest.
Arguments:
- attention: bfloat16 [256, 16384], P(None, 'wide'), may hold values from -6 to 6
- out_proj: bfloat16 [16384, 8192], P('wide', 'narrow'), may hold values from -0.0625 to 0.0625
- residual: bfloat16 [512, 8192], P('wide', 'narrow'), may hold values from -6 to 6
- dictionary: bfloat16 [2, 8192, 32768], P(None, 'narrow', 'wide'), may hold values from -0.046875 to 0.046875
- enc_bias: float32 [32768], P('wide'), may hold values from -3 to 3
- active: int32 [256, 32768], P(None, 'wide'), may hold values 0 or 1
Outputs:
- grad_dictionary: bfloat16 [2, 8192, 32768], P(None, 'narrow', 'wide')
- grad_bias: float32 [32768], P('wide')
All inputs are finite; a program needn't handle non-finite values. No bound on the sum of `active` on one device may be relied on, other than what follows from the above.
Results may differ from a plain program's by a relative error of at most 0.01.
Values may be sent and summed in bfloat16 or wider, within the bound.
A program may use at most 64 MiB of HBM per device.

v0:
```python
import jax
import jax.numpy as jnp
from jax import lax
from jax.sharding import PartitionSpec as P


def contract(left, right, left_dim, right_dim):
    return lax.dot_general(
        left, right, (((left_dim,), (right_dim,)), ((), ())), preferred_element_type=jnp.float32
    )


def body(attention, out_proj, residual, dictionary, enc_bias, active):
    wide_count = lax.axis_size("wide")
    position = lax.axis_index("wide")
    tokens = attention.shape[0]
    feat_split = out_proj.shape[1]
    own_rows = residual.shape[0]
    which_model = position // (wide_count // 2)
    partial_value = jnp.dot(attention, out_proj, preferred_element_type=jnp.float32)
    slots = jnp.zeros((2 * tokens, feat_split), jnp.float32)
    slots = lax.dynamic_update_slice_in_dim(slots, partial_value, which_model * tokens, 0)
    mine_rows = lax.dynamic_slice_in_dim(slots, position * own_rows, own_rows, 0)
    slots = lax.dynamic_update_slice_in_dim(
        slots, mine_rows + residual.astype(jnp.float32), position * own_rows, 0
    )
    stacked = lax.psum(slots, "wide").astype(jnp.bfloat16)
    fields = jnp.concatenate([stacked[:tokens], stacked[tokens:]], axis=1)
    flat_dict = dictionary.reshape(2 * feat_split, dictionary.shape[2])
    pre_part = jnp.dot(fields, flat_dict, preferred_element_type=jnp.float32)
    preact = lax.psum(pre_part, "narrow") + enc_bias
    active_f = active.astype(jnp.float32)
    features = (active_f * preact).astype(jnp.bfloat16)
    tok_rows = tokens // wide_count
    recon_own = lax.psum_scatter(
        contract(features, flat_dict, 1, 1), "wide", scatter_dimension=0, tiled=True
    )
    target = lax.dynamic_slice_in_dim(fields, position * tok_rows, tok_rows, 0)
    error_own = (recon_own - target.astype(jnp.float32)).astype(jnp.bfloat16)
    errors = lax.all_gather(error_own, "wide", axis=0, tiled=True)
    grad_part = jnp.dot(errors, flat_dict, preferred_element_type=jnp.float32)
    grad_features = lax.psum(grad_part, "narrow")
    grad_preact = (active_f * grad_features).astype(jnp.bfloat16)
    grad_bias = jnp.sum(grad_preact.astype(jnp.float32), axis=0)
    grad_total = contract(fields, grad_preact, 0, 0) + contract(errors, features, 0, 0)
    return (grad_total.astype(jnp.bfloat16).reshape(dictionary.shape), grad_bias)


def solution(mesh):
    in_specs = (
        P(None, "wide"),
        P("wide", "narrow"),
        P("wide", "narrow"),
        P(None, "narrow", "wide"),
        P("wide"),
        P(None, "wide"),
    )
    out_specs = (P(None, "narrow", "wide"), P("wide"))
    return jax.shard_map(body, mesh=mesh, in_specs=in_specs, out_specs=out_specs, check_vma=False)
```

profile of v0, /device:TPU:1, one launch (start us, length us, event | category | flops | bytes accessed | tf_op | source)
XLA Modules:
  0.0 1362.4 jit_solution(17609004116839913443)
XLA Ops:
  7.3 2.5 broadcast_in_dim.4
  9.8 1.8 convolution_dynamic-update-slice_fusion
  11.6 1.5 add_dynamic-update-slice_fusion
  13.0 359.4 %all-reduce.11 = bf16[512,2048]{1,0:T(8,128)(2,1)} all-reduce(f32[512,2048]{1,0:T(8,128)} %add_dynamic-update-slice_fusion), channel_id=1, replica_groups=mesh['wide'=64,'narrow'=4] {'wide'}, use_global_device_ids=true, to_apply=%region_0.1 | all-reduce | flops 1048576 | bytes 6291456 | tf_op jit(solution)/shard_map/psum | solution.py:27
  372.4 1.9 fusion.7
  374.3 0.9 copy-done.2
  375.2 2.0 fusion.1
  377.3 0.0 all-reduce.10.cloned.1.call-start
  377.3 88.4 %all-reduce.6.cloned.1.call-done = f32[256,512]{1,0:T(8,128)} async-done(((f32[256,512]{1,0:T(8,128)}), f32[256,512]{1,0:T(8,128)}) %all-reduce.6.cloned.1.call-update) | async-done | bytes 524304 | tf_op jit(solution)/shard_map/psum | solution.py:31
  465.8 1.3 multiply_convert_fusion.1
  467.1 5.5 fusion.8
  472.7 0.6 copy-done.6
  473.3 0.6 dynamic-slice
  474.5 659.1 %all-reduce.10.cloned.1.call-done = f32[256,4096]{1,0:T(8,128)} async-done(((f32[256,4096]{1,0:T(8,128)}), f32[256,4096]{1,0:T(8,128)}) %all-reduce.10.cloned.1.call-update) | async-done | bytes 4194320
  1133.6 1.6 fusion.4
  1135.2 0.0 all-reduce.8.cloned.1.call-start
  1135.2 161.7 %all-gather.3.cloned.1.call-done = bf16[64,4,4096]{2,1,0:T(4,128)(2,1)} async-done(((bf16[1,4,4096]{2,1,0:T(4,128)(2,1)}), bf16[64,4,4096]{2,1,0:T(4,128)(2,1)}) %all-gather.3.cloned.1.call-update) | async-done | bytes 2097168 | tf_op jit(solution)/shard_map/all_gather | solution.py:40
  1296.9 3.9 reshape.14
  1300.8 4.9 fusion.9
  1305.7 43.4 %all-reduce.8.cloned.1.call-done = f32[256,512]{1,0:T(8,128)} async-done(((f32[256,512]{1,0:T(8,128)}), f32[256,512]{1,0:T(8,128)}) %all-reduce.8.cloned.1.call-update) | async-done | bytes 524304 | tf_op jit(solution)/shard_map/psum | solution.py:42
  1349.1 1.9 convert_reduce_fusion
  1351.0 1.3 fusion
  1352.3 0.3 copy-done.1
  1352.6 3.3 add_convert_fusion
  (17 shorter events, 0.2 us)
Async XLA Ops:
  7.2 2.6 copy-start
  7.2 2.6 copy-start.3
  7.2 4.4 copy-start.4
  7.2 458.6 %all-reduce.6.cloned.1.call-start = ((), (), s32[]{:S(2)}) async-start(), calls=%async_computation | async-start | bytes 1048576 | tf_op jit(solution)/shard_map/psum | solution.py:31
  372.4 2.8 copy-start.2
  375.2 90.6 %copy-start.5 = (f32[512]{0:T(512)S(1)}, f32[512]{0:T(512)}, u32[]{:S(2)}) copy-start(f32[512]{0:T(512)} %param.10) | copy-start | bytes 6148
  377.3 756.3 %all-reduce.10.cloned.1.call-start = ((), (), s32[]{:S(2)}) async-start(), calls=%async_computation.3 | async-start | bytes 8388608
  472.6 0.7 copy-start.6
  472.6 824.2 %all-gather.3.cloned.1.call-start = ((), (), s32[]{:S(2)}) async-start(), calls=%async_computation.2 | async-start | bytes 2129920 | tf_op jit(solution)/shard_map/all_gather | solution.py:40
  1135.2 213.9 %all-reduce.8.cloned.1.call-start = ((), (), s32[]{:S(2)}) async-start(), calls=%async_computation.1 | async-start | bytes 1048576 | tf_op jit(solution)/shard_map/psum | solution.py:42
  1351.0 1.6 copy-start.1
Sparse Core Ops, SparseCore 0:
  377.4 88.3 all-reduce.5
  472.7 660.7 all-reduce.9
  1138.4 158.4 all-gather.2
  1305.8 43.2 all-reduce.7
where the time goes:
time: 1360 us
  waiting for transfers between devices  953 us (70%)
  blocking collectives  359 us (26%)
  matrix products  18.8 us (1%)
  between operations  14.5 us (1%)
    unnamed x5, waiting for transfers between devices  659 us
    psum x1, blocking collectives, body(): stacked = lax.psum(slots, 'wide').astype(jnp.bfloat16)  359 us
    all_gather x1, waiting for transfers between devices, body(): errors = lax.all_gather(error_own, 'wide', axis=0, tiled=True)  162 us
    psum x1, waiting for transfers between devices, body(): preact = lax.psum(pre_part, 'narrow') + enc_bias  88.4 us
    psum x1, waiting for transfers between devices, body(): grad_features = lax.psum(grad_part, 'narrow')  43.4 us
  transfers between devices with their start and end apart: 4, of which 4 were waited for; matrix products, arithmetic and copies ran while one was open for 0% of the time, Pallas kernels for 0%

commit v1 on v0

v1 whole, which is shorter than its diff:
```python
import jax
import jax.numpy as jnp
from jax import lax
from jax.experimental import pallas as pl
from jax.experimental.pallas import tpu as pltpu
from jax.sharding import PartitionSpec as P

MESH = pl.DeviceIdType.MESH
F32 = jnp.float32
BF16 = jnp.bfloat16
NX, NZ, NY = 2, 8, 4
ROWS = 16
CHUNK = NZ * ROWS
FEAT = 512
LAT = 512
SENDS = 101


def nt_dot(left, right):
    return lax.dot_general(left, right, (((1,), (1,)), ((), ())), preferred_element_type=F32)


def tn_dot(left, right):
    return lax.dot_general(left, right, (((0,), (0,)), ((), ())), preferred_element_type=F32)


def step_kernel(
    attn, proj, resid, dict_hbm, bias, act,
    fields, errors, feats, gpre,
    dic, dic_sem, res_out, res_in,
    proj_acc, proj_out, proj_in, fold_out, fold_in,
    pre, half_out, half_in, pair_out, pair_in,
    rec_out, rec_own, x_in, y_out, y_in, z_out, z_in,
    sq_in, sz_out, sz_in, sx_out, sx_in,
    send_sem, recv_sem,
):
    wide = lax.axis_index("wide")
    narrow = lax.axis_index("narrow")
    xh, z, y = wide // 32, (wide // 4) % 8, wide % 4
    xl, core = narrow // 2, narrow % 2

    def dev(xh_=xh, z_=z, y_=y, xl_=xl, core_=core):
        return ((xh_ * 8 + z_) * 4 + y_, xl_ * 2 + core_)

    x_peer = dev(xh_=1 - xh)
    pair_peer = dev(xl_=1 - xl)
    core_peer = dev(core_=1 - core)
    y_at = [(y + k) % 4 for k in range(4)]
    z_at = [(z + k) % 8 for k in range(8)]
    y_peer = [dev(y_=at) for at in y_at]
    z_peer = [dev(z_=at) for at in z_at]

    dict_copy = pltpu.make_async_copy(dict_hbm, dic, dic_sem)
    dict_copy.start()

    barrier = pltpu.get_barrier_semaphore()
    partners = [x_peer, pair_peer, core_peer] + y_peer[1:] + z_peer[1:]
    for peer in partners:
        pl.semaphore_signal(barrier, inc=1, device_id=peer, device_id_type=MESH)
    pl.semaphore_wait(barrier, len(partners))

    started = []

    def send(src, dst, peer):
        slot = len(started)
        copy = pltpu.make_async_remote_copy(
            src_ref=src, dst_ref=dst, send_sem=send_sem.at[slot], recv_sem=recv_sem.at[slot],
            device_id=peer, device_id_type=MESH,
        )
        copy.start()
        started.append(copy)
        return copy

    for k in range(4):
        at = y_at[k]
        cols = pl.ds(pl.multiple_of(at * FEAT, FEAT), FEAT)
        if k == 0:
            res_in[0] = resid[:, cols].astype(F32)
        else:
            res_out[k] = resid[:, cols].astype(F32)
    res_copies = [send(res_out.at[k], res_in.at[k], y_peer[k]) for k in range(1, 4)]
    res_waited = []

    def gather(ref, c, first):
        if first == "z":
            copies = [send(ref.at[xh, y, c, z], ref.at[xh, y, c, z], z_peer[k]) for k in range(1, 8)]
            yield
            for copy in copies:
                copy.wait_recv()
            copies = [send(ref.at[xh, y, c], ref.at[xh, y, c], y_peer[k]) for k in range(1, 4)]
            yield
            for copy in copies:
                copy.wait_recv()
            copy = send(ref.at[xh, :, c], ref.at[xh, :, c], x_peer)
            yield
            copy.wait_recv()
        else:
            copy = send(ref.at[xh, y, c, z], ref.at[xh, y, c, z], x_peer)
            yield
            copy.wait_recv()
            copies = [send(ref.at[:, y, c, z], ref.at[:, y, c, z], z_peer[k]) for k in range(1, 8)]
            yield
            for copy in copies:
                copy.wait_recv()
            copies = [send(ref.at[:, y, c], ref.at[:, y, c], y_peer[k]) for k in range(1, 4)]
            yield
            for copy in copies:
                copy.wait_recv()

    def encode(ref, c, result, stage, with_bias):
        pre[c, stage] = jnp.zeros((CHUNK, LAT), F32)

        def block(j, _):
            rows = ref[j // NY, j % NY, c].reshape(CHUNK, FEAT)
            pre[c, stage] += jnp.dot(rows, dic[j], preferred_element_type=F32)
            return 0

        lax.fori_loop(0, NX * NY, block, 0)
        mine = pl.ds(pl.multiple_of(core * 64, 64), 64)
        theirs = pl.ds(pl.multiple_of((1 - core) * 64, 64), 64)
        half_out[c, stage] = pre[c, stage, theirs, :].astype(BF16)
        copy = send(half_out.at[c, stage], half_in.at[c, stage], core_peer)
        yield
        copy.wait_recv()
        half = (pre[c, stage, mine, :] + half_in[c, stage].astype(F32)).astype(BF16)
        pair_out[c, stage] = half
        copy = send(pair_out.at[c, stage], pair_in.at[c, stage], pair_peer)
        yield
        copy.wait_recv()
        total = pair_out[c, stage].astype(F32) + pair_in[c, stage].astype(F32)
        if with_bias:
            total = total + bias[...]
        places = pl.ds(core * 4, 4)
        mask = act[places, c].reshape(64, LAT).astype(F32)
        result[c, places] = (mask * total).astype(BF16).reshape(4, ROWS, LAT)
        copy = send(result.at[c, places], result.at[c, places], core_peer)
        yield
        copy.wait_recv()

    def chain(c):
        rows = attn[:, c].reshape(CHUNK, 256)
        copies = []
        for k in (1, 3, 2, 0):
            cols = pl.ds(pl.multiple_of(y_at[k] * FEAT, FEAT), FEAT)
            part = jnp.dot(rows, proj[:, cols], preferred_element_type=F32).reshape(NZ, ROWS, FEAT)
            if k == 0:
                proj_acc[c] = part
            else:
                proj_out[c, k] = part.astype(BF16)
                copies.append(send(proj_out.at[c, k], proj_in.at[c, k], y_peer[k]))
        yield
        for copy in copies:
            copy.wait_recv()
        summed = proj_acc[c]
        for k in range(1, 4):
            summed = summed + proj_in[c, k].astype(F32)
        proj_acc[c] = summed
        fold_out[c] = summed.astype(BF16)
        copies = [send(fold_out.at[c, z_at[k]], fold_in.at[c, k], z_peer[k]) for k in range(1, 8)]
        yield
        if not res_waited:
            for copy in res_copies:
                copy.wait_recv()
            res_waited.append(True)
        for copy in copies:
            copy.wait_recv()
        own = proj_acc[c, z]
        for k in range(1, 8):
            own = own + fold_in[c, k].astype(F32)
        low = res_in[(y - 2 * c + 4) % 4]
        high = res_in[(y - 2 * c + 3) % 4]
        fields[xh, y, c, z] = (own + jnp.concatenate([low, high], axis=0)).astype(BF16)
        yield from gather(fields, c, "z" if c == 0 else "x")
        if c == 0:
            dict_copy.wait()
        yield from encode(fields, c, feats, 0, True)

        code = feats[c].reshape(CHUNK, LAT)
        if c == 0:
            def other(j, _):
                rec_out[0, j] = nt_dot(code, dic[(1 - xh) * NY + j]).astype(BF16).reshape(NZ, ROWS, FEAT)
                return 0

            lax.fori_loop(0, NY, other, 0)
            copy = send(rec_out.at[0, pl.ds(0, 4)], x_in, x_peer)

            def mine(j, _):
                rec_own[0, j] = nt_dot(code, dic[xh * NY + j]).reshape(NZ, ROWS, FEAT)
                return 0

            lax.fori_loop(0, NY, mine, 0)
            yield
            copy.wait_recv()
            copies = []
            for k in (1, 3, 2, 0):
                at = y_at[k]
                part = rec_own[0, at] + x_in[at].astype(F32)
                if k == 0:
                    rec_own[0, at] = part
                else:
                    y_out[k] = part.astype(BF16)
                    copies.append(send(y_out.at[k], y_in.at[k], y_peer[k]))
            yield
            for copy in copies:
                copy.wait_recv()
            part = rec_own[0, y]
            for k in range(1, 4):
                part = part + y_in[k].astype(F32)
            rec_own[0, y] = part
            z_out[...] = part.astype(BF16)
            copies = [send(z_out.at[z_at[k]], z_in.at[k], z_peer[k]) for k in range(1, 8)]
            yield
            for copy in copies:
                copy.wait_recv()
            recon = rec_own[0, y, z]
            for k in range(1, 8):
                recon = recon + z_in[k].astype(F32)
        else:
            copies = []
            for k in (1, 3, 2, 0):
                at = y_at[k]
                for m in range(NX):
                    part = nt_dot(code, dic[m * NY + at]).reshape(NZ, ROWS, FEAT)
                    if k == 0:
                        rec_own[1, m] = part
                    else:
                        rec_out[1, 2 * (k - 1) + m] = part.astype(BF16)
                if k:
                    copies.append(send(rec_out.at[1, pl.ds(2 * (k - 1), 2)], sq_in.at[k], y_peer[k]))
            yield
            for copy in copies:
                copy.wait_recv()
            for m in range(NX):
                part = rec_own[1, m]
                for k in range(1, 4):
                    part = part + sq_in[k, m].astype(F32)
                rec_own[1, m] = part
                sz_out[m] = part.astype(BF16)
            copies = [send(sz_out.at[:, z_at[k]], sz_in.at[k], z_peer[k]) for k in range(1, 8)]
            yield
            for copy in copies:
                copy.wait_recv()
            part = rec_own[1, 1 - xh, z]
            for k in range(1, 8):
                part = part + sz_in[k, 1 - xh].astype(F32)
            sx_out[...] = part.astype(BF16)
            copy = send(sx_out, sx_in, x_peer)
            recon = rec_own[1, xh, z]
            for k in range(1, 8):
                recon = recon + sz_in[k, xh].astype(F32)
            rec_own[1, 2, 0] = recon
            yield
            copy.wait_recv()
            recon = rec_own[1, 2, 0] + sx_in[...].astype(F32)
        errors[xh, y, c, z] = (recon - fields[xh, y, c, z].astype(F32)).astype(BF16)
        yield from gather(errors, c, "z" if c == 0 else "x")
        yield from encode(errors, c, gpre, 1, False)

    running = [chain(0), chain(1)]
    while running:
        for one in list(running):
            if next(one, "end") == "end":
                running.remove(one)
    for copy in started:
        copy.wait_send()


def gradient_kernel(fields, errors, feats, gpre, grad, bias_grad):
    code = feats[...]
    slope = gpre[...]
    grad[...] = (tn_dot(fields[...], slope) + tn_dot(errors[...], code)).astype(BF16)

    @pl.when(pl.program_id(0) == 0)
    def _():
        bias_grad[...] = jnp.sum(slope.astype(F32), axis=0, keepdims=True)


def body(attention, out_proj, residual, dictionary, enc_bias, active):
    vmem = pl.BlockSpec(memory_space=pltpu.VMEM)
    piece = (NX, NY, 2, NZ, ROWS, FEAT)
    code = (2, NZ, ROWS, LAT)
    shapes = [piece, piece, code, code]
    fields, errors, feats, gpre = pl.pallas_call(
        step_kernel,
        out_shape=[jax.ShapeDtypeStruct(s, BF16) for s in shapes],
        in_specs=[vmem, vmem, vmem, pl.BlockSpec(memory_space=pl.ANY), vmem, vmem],
        out_specs=[vmem] * 4,
        scratch_shapes=[
            pltpu.VMEM((NX * NY, FEAT, LAT), BF16),
            pltpu.SemaphoreType.DMA,
            pltpu.VMEM((4, 8, FEAT), F32),
            pltpu.VMEM((4, 8, FEAT), F32),
            pltpu.VMEM((2, NZ, ROWS, FEAT), F32),
            pltpu.VMEM((2, 4, NZ, ROWS, FEAT), BF16),
            pltpu.VMEM((2, 4, NZ, ROWS, FEAT), BF16),
            pltpu.VMEM((2, NZ, ROWS, FEAT), BF16),
            pltpu.VMEM((2, 8, ROWS, FEAT), BF16),
            pltpu.VMEM((2, 2, CHUNK, LAT), F32),
            pltpu.VMEM((2, 2, 64, LAT), BF16),
            pltpu.VMEM((2, 2, 64, LAT), BF16),
            pltpu.VMEM((2, 2, 64, LAT), BF16),
            pltpu.VMEM((2, 2, 64, LAT), BF16),
            pltpu.VMEM((2, 6, NZ, ROWS, FEAT), BF16),
            pltpu.VMEM((2, 4, NZ, ROWS, FEAT), F32),
            pltpu.VMEM((4, NZ, ROWS, FEAT), BF16),
            pltpu.VMEM((4, NZ, ROWS, FEAT), BF16),
            pltpu.VMEM((4, NZ, ROWS, FEAT), BF16),
            pltpu.VMEM((NZ, ROWS, FEAT), BF16),
            pltpu.VMEM((8, ROWS, FEAT), BF16),
            pltpu.VMEM((4, 2, NZ, ROWS, FEAT), BF16),
            pltpu.VMEM((2, NZ, ROWS, FEAT), BF16),
            pltpu.VMEM((8, 2, ROWS, FEAT), BF16),
            pltpu.VMEM((ROWS, FEAT), BF16),
            pltpu.VMEM((ROWS, FEAT), BF16),
            pltpu.SemaphoreType.DMA((SENDS,)),
            pltpu.SemaphoreType.DMA((SENDS,)),
        ],
        compiler_params=pltpu.CompilerParams(
            collective_id=0, has_side_effects=True, vmem_limit_bytes=48 << 20
        ),
        name="crosscoder_step",
    )(
        attention.reshape(NZ, 2, ROWS, 256),
        out_proj,
        residual,
        dictionary.reshape(NX * NY, FEAT, LAT),
        enc_bias.reshape(1, LAT),
        active.reshape(NZ, 2, ROWS, LAT),
    )
    block = pl.BlockSpec((None, 2 * CHUNK, FEAT), lambda j: (j, 0, 0))
    whole = pl.BlockSpec((2 * CHUNK, LAT), lambda j: (0, 0))
    grad, bias_grad = pl.pallas_call(
        gradient_kernel,
        grid=(NX * NY,),
        out_shape=[
            jax.ShapeDtypeStruct((NX * NY, FEAT, LAT), BF16),
            jax.ShapeDtypeStruct((1, LAT), F32),
        ],
        in_specs=[block, block, whole, whole],
        out_specs=[
            pl.BlockSpec((None, FEAT, LAT), lambda j: (j, 0, 0)),
            pl.BlockSpec((1, LAT), lambda j: (0, 0)),
        ],
        compiler_params=pltpu.CompilerParams(vmem_limit_bytes=32 << 20),
        name="dictionary_gradient",
    )(
        fields.reshape(NX * NY, 2 * CHUNK, FEAT),
        errors.reshape(NX * NY, 2 * CHUNK, FEAT),
        feats.reshape(2 * CHUNK, LAT),
        gpre.reshape(2 * CHUNK, LAT),
    )
    return grad.reshape(dictionary.shape), bias_grad.reshape(LAT)


def solution(mesh):
    in_specs = (
        P(None, "wide"),
        P("wide", "narrow"),
        P("wide", "narrow"),
        P(None, "narrow", "wide"),
        P("wide"),
        P(None, "wide"),
    )
    out_specs = (P(None, "narrow", "wide"), P("wide"))
    return jax.shard_map(body, mesh=mesh, in_specs=in_specs, out_specs=out_specs, check_vma=False)
```

time: 1360 us -> 137 us (0.10)
  waiting for transfers between devices: 953 us -> 0 us
  blocking collectives: 359 us -> 0 us
  Pallas kernels: 0 us -> 130 us
  matrix products: 18.8 us -> 0 us
  between operations: 14.5 us -> 0.66 us
    unnamed x5 -> x0, waiting for transfers between devices: 659 us -> none
    psum x1 -> x0, blocking collectives: 359 us -> none  [body(): stacked = lax.psum(slots, 'wide').astype(jnp.bfloat16)]
    all_gather x1 -> x0, waiting for transfers between devices: 162 us -> none  [body(): errors = lax.all_gather(error_own, 'wide', axis=0, tiled=True)]
    psum x2 -> x0, waiting for transfers between devices: 132 us -> none  [the longest x1 88.4 us: body(): preact = lax.psum(pre_part, 'narrow') + enc_bias]
    pallas_call x0 -> x2, Pallas kernels: none -> 130 us  [the longest x1 124 us: body(): pl.pallas_call(step_kernel, out_shape=[jax.ShapeDtypeStruct(s, BF16) for...]
    dot_general x6 -> x0, matrix products: 18.8 us -> none  [the longest x3 10.1 us: contract(): lax.dot_general(left, right, (((left_dim,), (right_dim,)), ((), ())), pre...]
  transfers between devices with their start and end apart: 4 -> 0, of which waited for: 4 -> 0; matrix products, arithmetic and copies ran while one was open for 0% -> 0% of each run, Pallas kernels for 0% -> 0%
where the time goes in v1:
time: 137 us
  Pallas kernels  130 us (95%)
  local copies, waits for them, and re-layouts  6.19 us (5%)
    pallas_call x1, Pallas kernels, body(): pl.pallas_call(step_kernel, out_shape=[jax.ShapeDtypeStruct(s, BF16) for...  124 us
    unnamed x12, local copies, waits for them, and re-layouts  6.19 us
    pallas_call x1, Pallas kernels, body(): pl.pallas_call(gradient_kernel, grid=(NX * NY,), out_shape=[jax.ShapeDtyp...  5.63 us

profile of v1, /device:TPU:1, one launch (start us, length us, event | category | flops | bytes accessed | tf_op | source)
XLA Modules:
  0.0 136.8 jit_solution(580762697087666763)
XLA Ops:
  0.6 0.0 copy-start.1
  0.6 1.2 copy-done.1
  1.9 0.0 copy-start.2
  1.9 1.0 copy-done.2
  2.9 0.0 copy-start.3
  2.9 0.9 copy-done.3
  3.8 0.0 copy-start.4
  3.8 0.8 copy-done.4
  4.6 0.0 copy-start.5
  4.6 0.7 copy-done.5
  5.2 124.4 %crosscoder_step.1 = (bf16[2,4,2,8,16,512]{5,4,3,2,1,0:T(8,128)(2,1)S(1)}, bf16[2,4,2,8,16,512]{5,4,3,2,1,0:T(8,128)(2,1)}, bf16[2,8,16,512]{3,2,1,0:T(8,128)(2,1)S(1)}, bf16[2,8,16,512]{3,2,1,0:T(8,128)(2,1)S(1)}) custom-call(bf16[8,2,16,256]{3,2,1,0:T(8,128)(2,1)S(1)} %bitcast.15, bf16[256,2048]{1,0:T(8,128)(2,1)S(1)} %copy-done.1, ...), custom_call_target="tpu_custom_call" | custom-call | tf_op jit(solution)/shard_map/crosscoder_step/pallas_call | solution.py:283
  129.6 0.0 copy-start
  129.6 1.6 %copy-done = bf16[2,4,2,8,16,512]{5,4,3,2,1,0:T(8,128)(2,1)S(1)} copy-done((bf16[2,4,2,8,16,512]{5,4,3,2,1,0:T(8,128)(2,1)S(1)}, bf16[2,4,2,8,16,512]{5,4,3,2,1,0:T(8,128)(2,1)}, u32[]{:S(2)}) %copy-start) | copy-done | bytes 2097176
  131.2 5.6 %dictionary_gradient.1 = (bf16[8,512,512]{2,1,0:T(8,128)(2,1)}, f32[1,512]{1,0:T(1,128)}) custom-call(bf16[8,256,512]{2,1,0:T(8,128)(2,1)S(1)} %bitcast.10, bf16[8,256,512]{2,1,0:T(8,128)(2,1)S(1)} %bitcast.11, bf16[256,512]{1,0:T(8,128)(2,1)S(1)} %bitcast.13, bf16[256,512]{1,0:T(8,128)(2,1)S(1)} %bitcast.14), custom_call_target="tpu_custom_call" | custom-call | tf_op jit(solution)/shard_map/dictionary_gradient/pallas_call | solution.py:332
Async XLA Ops:
  0.6 1.2 copy-start.1
  1.9 1.0 copy-start.2
  2.9 0.9 copy-start.3
  3.8 0.8 copy-start.4
  4.6 0.7 copy-start.5
  129.6 1.6 %copy-start = (bf16[2,4,2,8,16,512]{5,4,3,2,1,0:T(8,128)(2,1)S(1)}, bf16[2,4,2,8,16,512]{5,4,3,2,1,0:T(8,128)(2,1)}, u32[]{:S(2)}) copy-start(bf16[2,4,2,8,16,512]{5,4,3,2,1,0:T(8,128)(2,1)} %get-tuple-element.9) | copy-start | bytes 6291460

commit v2 on v1

v2 whole, which is shorter than its diff:
```python
import jax
import jax.numpy as jnp
from jax import lax
from jax.experimental import pallas as pl
from jax.experimental.pallas import tpu as pltpu
from jax.sharding import PartitionSpec as P

MESH = pl.DeviceIdType.MESH
F32 = jnp.float32
BF16 = jnp.bfloat16
NX, NZ, NY = 2, 8, 4
ROWS = 16
CHUNK = NZ * ROWS
FEAT = 512
LAT = 512
SENDS = 125
HALF = 256
DELAY = 1


def nt_dot(left, right):
    return lax.dot_general(left, right, (((1,), (1,)), ((), ())), preferred_element_type=F32)


def tn_dot(left, right):
    return lax.dot_general(left, right, (((0,), (0,)), ((), ())), preferred_element_type=F32)


def step_kernel(
    attn_hbm, proj_hbm, resid_hbm, dict_hbm, bias_hbm, act_hbm,
    turned_hbm, feats_hbm, gpre_hbm,
    turned, attn, proj, resid, dic, bias, act, fields, errors, feats, gpre,
    res_out, res_in,
    proj_acc, proj_out, proj_in, fold_out, fold_in,
    pre, half_out, half_in, pair_out, pair_in,
    xa_out, xa_in, xa_own, ya_out, ya_in,
    yb_out, yb_in, yb_own, xb_out, xb_in,
    z_own, z_out, z_in,
    local_sem, send_sem, recv_sem,
):
    wide = lax.axis_index("wide")
    narrow = lax.axis_index("narrow")
    xh, z, y = wide // 32, (wide // 4) % 8, wide % 4
    xl, core = narrow // 2, narrow % 2

    def dev(xh_=xh, z_=z, y_=y, xl_=xl, core_=core):
        return ((xh_ * 8 + z_) * 4 + y_, xl_ * 2 + core_)

    x_peer = dev(xh_=1 - xh)
    pair_peer = dev(xl_=1 - xl)
    core_peer = dev(core_=1 - core)
    y_at = [(y + k) % 4 for k in range(4)]
    z_at = [(z + k) % 8 for k in range(8)]
    y_peer = [dev(y_=at) for at in y_at]
    z_peer = [dev(z_=at) for at in z_at]

    barrier = pltpu.get_barrier_semaphore()
    partners = [x_peer, pair_peer, core_peer] + y_peer[1:] + z_peer[1:]
    for peer in partners:
        pl.semaphore_signal(barrier, inc=1, device_id=peer, device_id_type=MESH)

    loads = []
    for src, dst in (
        (attn_hbm, attn), (proj_hbm, proj), (resid_hbm, resid),
        (bias_hbm, bias), (act_hbm, act), (dict_hbm, dic),
    ):
        copy = pltpu.make_async_copy(src, dst, local_sem.at[len(loads)])
        copy.start()
        loads.append(copy)

    started = []
    stores = []

    def send(src, dst, peer):
        slot = len(started)
        copy = pltpu.make_async_remote_copy(
            src_ref=src, dst_ref=dst, send_sem=send_sem.at[slot], recv_sem=recv_sem.at[slot],
            device_id=peer, device_id_type=MESH,
        )
        copy.start()
        started.append(copy)
        return copy

    def store(src, dst):
        copy = pltpu.make_async_copy(src, dst, local_sem.at[len(loads) + len(stores)])
        copy.start()
        stores.append(copy)

    low, high = pl.ds(0, HALF), pl.ds(HALF, HALF)
    z_order = (4, 3, 5, 2, 6, 1, 7)
    y_order = (2, 1, 3)

    def gather(ref, c):
        copies = [send(ref.at[xh, y, c, z], ref.at[xh, y, c, z], z_peer[k]) for k in z_order]
        yield
        for copy in copies:
            copy.wait_recv()
        along = ref.at[xh, y, c, :, :, high]
        copies = [send(along, along, x_peer)]
        along = ref.at[xh, y, c, :, :, low]
        copies += [send(along, along, y_peer[k]) for k in y_order]
        yield
        for copy in copies[1:]:
            copy.wait_recv()
        along = ref.at[xh, :, c, :, :, low]
        last = [send(along, along, x_peer)]
        copies[0].wait_recv()
        along = ref.at[:, y, c, :, :, high]
        last += [send(along, along, y_peer[k]) for k in y_order]
        yield
        for copy in last:
            copy.wait_recv()

    def turn(ref, c, stage, blocks):
        for j in blocks:
            turned[stage, c, j] = ref[j // NY, j % NY, c].reshape(CHUNK, FEAT).T

    def encode(ref, c, result, stage, with_bias):
        total = None
        for m in range(NX):
            for at in range(NY):
                part = jnp.dot(ref[m, at, c].reshape(CHUNK, FEAT), dic[m * NY + at], preferred_element_type=F32)
                total = part if total is None else total + part
        pre[c, stage] = total
        mine = pl.ds(pl.multiple_of(core * 64, 64), 64)
        theirs = pl.ds(pl.multiple_of((1 - core) * 64, 64), 64)
        half_out[c, stage] = pre[c, stage, theirs, :].astype(BF16)
        copy = send(half_out.at[c, stage], half_in.at[c, stage], core_peer)
        turn(ref, c, stage, (0, 1))
        yield
        copy.wait_recv()
        half = (pre[c, stage, mine, :] + half_in[c, stage].astype(F32)).astype(BF16)
        pair_out[c, stage] = half
        copy = send(pair_out.at[c, stage], pair_in.at[c, stage], pair_peer)
        turn(ref, c, stage, range(2, NX * NY))
        store(turned.at[stage, c], turned_hbm.at[stage, c])
        yield
        copy.wait_recv()
        total = pair_out[c, stage].astype(F32) + pair_in[c, stage].astype(F32)
        if with_bias:
            total = total + bias[...]
        places = pl.ds(core * 4, 4)
        mask = act[places, c].reshape(64, LAT).astype(F32)
        result[c, places] = (mask * total).astype(BF16).reshape(4, ROWS, LAT)
        copy = send(result.at[c, places], result.at[c, places], core_peer)
        yield
        copy.wait_recv()

    def project(c):
        rows = attn[:, c].reshape(CHUNK, 256)
        for k in y_order + (0,):
            cols = pl.ds(pl.multiple_of(y_at[k] * FEAT, FEAT), FEAT)
            part = jnp.dot(rows, proj[:, cols], preferred_element_type=F32).reshape(NZ, ROWS, FEAT)
            if k == 0:
                proj_acc[c] = part
            else:
                proj_out[c, k] = part.astype(BF16)

    def chain(c):
        copies = [send(proj_out.at[c, k], proj_in.at[c, k], y_peer[k]) for k in y_order]
        yield
        for copy in copies:
            copy.wait_recv()
        summed = proj_acc[c]
        for k in range(1, 4):
            summed = summed + proj_in[c, k].astype(F32)
        proj_acc[c] = summed
        fold_out[c] = summed.astype(BF16)
        copies = [send(fold_out.at[c, z_at[k]], fold_in.at[c, k], z_peer[k]) for k in z_order]
        yield
        if c == 0:
            for copy in res_copies:
                copy.wait_recv()
        for copy in copies:
            copy.wait_recv()
        own = proj_acc[c, z]
        for k in range(1, 8):
            own = own + fold_in[c, k].astype(F32)
        upper = res_in[(y - 2 * c + 4) % 4]
        lower = res_in[(y - 2 * c + 3) % 4]
        fields[xh, y, c, z] = (own + jnp.concatenate([upper, lower], axis=0)).astype(BF16)
        yield from gather(fields, c)
        if c == 0:
            for copy in loads[3:]:
                copy.wait()
        yield from encode(fields, c, feats, 0, True)
        store(feats.at[c], feats_hbm.at[c])

        code = feats[c].reshape(CHUNK, LAT)

        def decode(j, cols):
            return nt_dot(code, dic[j, cols, :]).reshape(NZ, ROWS, HALF)

        for at in range(NY):
            xa_out[c, at] = decode((1 - xh) * NY + at, low).astype(BF16)
        xa_copy = send(xa_out.at[c], xa_in.at[c], x_peer)
        yb_copies = []
        for k in y_order:
            for m in range(NX):
                yb_out[c, k, m] = decode(m * NY + y_at[k], high).astype(BF16)
            yb_copies.append(send(yb_out.at[c, k], yb_in.at[c, k], y_peer[k]))
        for at in range(NY):
            xa_own[c, at] = decode(xh * NY + at, low)
        for m in range(NX):
            yb_own[c, m] = decode(m * NY + y, high)
        yield
        xa_copy.wait_recv()
        ya_copies = []
        for k in y_order + (0,):
            at = y_at[k]
            part = xa_own[c, at] + xa_in[c, at].astype(F32)
            if k == 0:
                z_own[c, :, :, :HALF] = part
            else:
                ya_out[c, k] = part.astype(BF16)
                ya_copies.append(send(ya_out.at[c, k], ya_in.at[c, k], y_peer[k]))
        for copy in yb_copies:
            copy.wait_recv()

        def over_y(m):
            part = yb_own[c, m]
            for k in range(1, 4):
                part = part + yb_in[c, k, m].astype(F32)
            return part

        xb_out[c] = over_y(1 - xh).astype(BF16)
        xb_copy = send(xb_out.at[c], xb_in.at[c], x_peer)
        z_own[c, :, :, HALF:] = over_y(xh)
        yield
        for copy in ya_copies:
            copy.wait_recv()
        part = z_own[c, :, :, :HALF]
        for k in range(1, 4):
            part = part + ya_in[c, k].astype(F32)
        z_own[c, :, :, :HALF] = part
        z_out[c, :, :, :HALF] = part.astype(BF16)
        xb_copy.wait_recv()
        part = z_own[c, :, :, HALF:] + xb_in[c].astype(F32)
        z_own[c, :, :, HALF:] = part
        z_out[c, :, :, HALF:] = part.astype(BF16)
        copies = [send(z_out.at[c, z_at[k]], z_in.at[c, k], z_peer[k]) for k in z_order]
        yield
        for copy in copies:
            copy.wait_recv()
        recon = z_own[c, z]
        for k in range(1, 8):
            recon = recon + z_in[c, k].astype(F32)
        errors[xh, y, c, z] = (recon - fields[xh, y, c, z].astype(F32)).astype(BF16)
        yield from gather(errors, c)
        yield from encode(errors, c, gpre, 1, False)
        store(gpre.at[c], gpre_hbm.at[c])

    for copy in loads[:2]:
        copy.wait()
    project(0)
    loads[2].wait()
    for k in range(4):
        cols = pl.ds(pl.multiple_of(y_at[k] * FEAT, FEAT), FEAT)
        if k == 0:
            res_in[0] = resid[:, cols].astype(F32)
        else:
            res_out[k] = resid[:, cols].astype(F32)
    pl.semaphore_wait(barrier, len(partners))
    first, second = chain(0), chain(1)
    next(first)
    res_copies = [send(res_out.at[k], res_in.at[k], y_peer[k]) for k in y_order]
    project(1)
    for _ in range(DELAY):
        next(first)
    running = [second, first]
    while running:
        for one in list(running):
            if next(one, "end") == "end":
                running.remove(one)
    for copy in started:
        copy.wait_send()
    for copy in stores:
        copy.wait()


def gradient_kernel(
    turned_hbm, feats_hbm, gpre_hbm, grad_hbm, bias_grad, turned, code, grad, code_sem, in_sem, out_sem
):
    first = [
        pltpu.make_async_copy(gpre_hbm, code.at[0], code_sem.at[0]),
        pltpu.make_async_copy(feats_hbm, code.at[1], code_sem.at[1]),
    ]
    blocks = [
        pltpu.make_async_copy(turned_hbm.at[:, :, j], turned.at[:, :, j], in_sem.at[j]) for j in range(NX * NY)
    ]
    for copy in first + blocks:
        copy.start()
    for copy in first:
        copy.wait()
    right = code[...].reshape(4 * CHUNK, LAT)
    stores = []
    for j in range(NX * NY):
        blocks[j].wait()
        left = jnp.concatenate([turned[s, c, j] for s in range(2) for c in range(2)], axis=1)
        grad[j] = jnp.dot(left, right, preferred_element_type=F32).astype(BF16)
        copy = pltpu.make_async_copy(grad.at[j], grad_hbm.at[j], out_sem.at[j])
        copy.start()
        stores.append(copy)
    bias_grad[...] = jnp.sum(code[0].astype(F32).reshape(2 * CHUNK, LAT), axis=0, keepdims=True)
    for copy in stores:
        copy.wait()


def body(attention, out_proj, residual, dictionary, enc_bias, active):
    hbm = pl.BlockSpec(memory_space=pl.ANY)
    piece = (NX, NY, 2, NZ, ROWS, FEAT)
    code = (2, NZ, ROWS, LAT)
    half = (NZ, ROWS, HALF)
    flipped = (2, 2, NX * NY, FEAT, CHUNK)
    shapes = [flipped, code, code]
    turned, feats, gpre = pl.pallas_call(
        step_kernel,
        out_shape=[jax.ShapeDtypeStruct(s, BF16) for s in shapes],
        in_specs=[hbm] * 6,
        out_specs=[hbm] * 3,
        scratch_shapes=[
            pltpu.VMEM(flipped, BF16),
            pltpu.VMEM((NZ, 2, ROWS, 256), BF16),
            pltpu.VMEM((256, NY * FEAT), BF16),
            pltpu.VMEM((8, NY * FEAT), BF16),
            pltpu.VMEM((NX * NY, FEAT, LAT), BF16),
            pltpu.VMEM((1, LAT), F32),
            pltpu.VMEM((NZ, 2, ROWS, LAT), jnp.int32),
            pltpu.VMEM(piece, BF16),
            pltpu.VMEM(piece, BF16),
            pltpu.VMEM(code, BF16),
            pltpu.VMEM(code, BF16),
            pltpu.VMEM((4, 8, FEAT), F32),
            pltpu.VMEM((4, 8, FEAT), F32),
            pltpu.VMEM((2, NZ, ROWS, FEAT), F32),
            pltpu.VMEM((2, 4, NZ, ROWS, FEAT), BF16),
            pltpu.VMEM((2, 4, NZ, ROWS, FEAT), BF16),
            pltpu.VMEM((2, NZ, ROWS, FEAT), BF16),
            pltpu.VMEM((2, 8, ROWS, FEAT), BF16),
            pltpu.VMEM((2, 2, CHUNK, LAT), F32),
            pltpu.VMEM((2, 2, 64, LAT), BF16),
            pltpu.VMEM((2, 2, 64, LAT), BF16),
            pltpu.VMEM((2, 2, 64, LAT), BF16),
            pltpu.VMEM((2, 2, 64, LAT), BF16),
            pltpu.VMEM((2, NY) + half, BF16),
            pltpu.VMEM((2, NY) + half, BF16),
            pltpu.VMEM((2, NY) + half, F32),
            pltpu.VMEM((2, 4) + half, BF16),
            pltpu.VMEM((2, 4) + half, BF16),
            pltpu.VMEM((2, 4, NX) + half, BF16),
            pltpu.VMEM((2, 4, NX) + half, BF16),
            pltpu.VMEM((2, NX) + half, F32),
            pltpu.VMEM((2,) + half, BF16),
            pltpu.VMEM((2,) + half, BF16),
            pltpu.VMEM((2, NZ, ROWS, FEAT), F32),
            pltpu.VMEM((2, NZ, ROWS, FEAT), BF16),
            pltpu.VMEM((2, 8, ROWS, FEAT), BF16),
            pltpu.SemaphoreType.DMA((14,)),
            pltpu.SemaphoreType.DMA((SENDS,)),
            pltpu.SemaphoreType.DMA((SENDS,)),
        ],
        compiler_params=pltpu.CompilerParams(
            collective_id=0, has_side_effects=True, vmem_limit_bytes=60 << 20
        ),
        name="crosscoder_step",
    )(
        attention.reshape(NZ, 2, ROWS, 256),
        out_proj,
        residual,
        dictionary.reshape(NX * NY, FEAT, LAT),
        enc_bias.reshape(1, LAT),
        active.reshape(NZ, 2, ROWS, LAT),
    )
    grad, bias_grad = pl.pallas_call(
        gradient_kernel,
        out_shape=[
            jax.ShapeDtypeStruct((NX * NY, FEAT, LAT), BF16),
            jax.ShapeDtypeStruct((1, LAT), F32),
        ],
        in_specs=[hbm] * 3,
        out_specs=[hbm, pl.BlockSpec(memory_space=pltpu.VMEM)],
        scratch_shapes=[
            pltpu.VMEM(flipped, BF16),
            pltpu.VMEM((2,) + code, BF16),
            pltpu.VMEM((NX * NY, FEAT, LAT), BF16),
            pltpu.SemaphoreType.DMA((2,)),
            pltpu.SemaphoreType.DMA((NX * NY,)),
            pltpu.SemaphoreType.DMA((NX * NY,)),
        ],
        compiler_params=pltpu.CompilerParams(vmem_limit_bytes=60 << 20),
        name="dictionary_gradient",
    )(turned, feats, gpre)
    return grad.reshape(dictionary.shape), bias_grad.reshape(LAT)


def solution(mesh):
    in_specs = (
        P(None, "wide"),
        P("wide", "narrow"),
        P("wide", "narrow"),
        P(None, "narrow", "wide"),
        P("wide"),
        P(None, "wide"),
    )
    out_specs = (P(None, "narrow", "wide"), P("wide"))
    return jax.shard_map(body, mesh=mesh, in_specs=in_specs, out_specs=out_specs, check_vma=False)
```

time: 137 us -> 117 us (0.85)
  Pallas kernels: 130 us -> 116 us
  local copies, waits for them, and re-layouts: 6.19 us -> 0 us
    pallas_call x1, Pallas kernels: 124 us -> 109 us  [body(): pl.pallas_call(step_kernel, out_shape=[jax.ShapeDtypeStruct(s, BF16) for...]
    unnamed x12 -> x0, local copies, waits for them, and re-layouts: 6.19 us -> none
    pallas_call x1, Pallas kernels: 5.63 us -> 7.2 us  [body(): pl.pallas_call(gradient_kernel, out_shape=[jax.ShapeDtypeStruct((NX * NY,...]
where the time goes in v2:
time: 117 us
  Pallas kernels  116 us (99%)
    pallas_call x1, Pallas kernels, body(): pl.pallas_call(step_kernel, out_shape=[jax.ShapeDtypeStruct(s, BF16) for...  109 us
    pallas_call x1, Pallas kernels, body(): pl.pallas_call(gradient_kernel, out_shape=[jax.ShapeDtypeStruct((NX * NY,...  7.2 us

profile of v2, /device:TPU:1, one launch (start us, length us, event | category | flops | bytes accessed | tf_op | source)
XLA Modules:
  0.0 117.1 jit_solution(9223092479588555681)
XLA Ops:
  0.6 109.2 %crosscoder_step.1 = (bf16[2,2,8,512,128]{4,3,2,1,0:T(8,128)(2,1)}, bf16[2,8,16,512]{3,2,1,0:T(8,128)(2,1)}, bf16[2,8,16,512]{3,2,1,0:T(8,128)(2,1)}) custom-call(bf16[8,2,16,256]{3,2,1,0:T(8,128)(2,1)} %bitcast.8, bf16[256,2048]{1,0:T(8,128)(2,1)} %proj_hbm.1, bf16[8,2048]{1,0:T(8,128)(2,1)} %resid_hbm.1, bf16[8,512,512]{2,1,0:T(8,128)(2,1)} %bitcast.6, ...), custom_call_target="tpu_custom_call" | custom-call | tf_op jit(solution)/shard_map/crosscoder_step/pallas_call | solution.py:316
  109.9 7.2 %dictionary_gradient.1 = (bf16[8,512,512]{2,1,0:T(8,128)(2,1)}, f32[1,512]{1,0:T(1,128)}) custom-call(bf16[2,2,8,512,128]{4,3,2,1,0:T(8,128)(2,1)} %get-tuple-element.7.turned_hbm, bf16[2,8,16,512]{3,2,1,0:T(8,128)(2,1)} %get-tuple-element.8.feats_hbm, bf16[2,8,16,512]{3,2,1,0:T(8,128)(2,1)} %get-tuple-element.9.gpre_hbm), custom_call_target="tpu_custom_call" | custom-call | tf_op jit(solution)/shard_map/dictionary_gradient/pallas_call | solution.py:374

commit v3 on v2

--- a/solution.py
+++ b/solution.py
@@ -13,7 +13,8 @@
 CHUNK = NZ * ROWS
 FEAT = 512
 LAT = 512
-SENDS = 125
+SENDS = 47
+LATE = 46
 HALF = 256
 DELAY = 1
 
@@ -68,18 +69,36 @@
         copy.start()
         loads.append(copy)
 
-    started = []
+    groups = []
     stores = []
 
+    class Group:
+        def __init__(self, size, copies):
+            slot = len(groups)
+            self.size, self.sems, self.sent = size, (send_sem.at[slot], recv_sem.at[slot]), False
+            for src, dst, peer in copies:
+                pltpu.make_async_remote_copy(
+                    src_ref=src, dst_ref=dst, send_sem=self.sems[0], recv_sem=self.sems[1],
+                    device_id=peer, device_id_type=MESH,
+                ).start()
+            groups.append(self)
+
+        def wait_recv(self):
+            pltpu.make_async_copy(self.size, self.size, self.sems[1]).wait()
+
+        def wait_send(self):
+            if not self.sent:
+                pltpu.make_async_copy(self.size, self.size, self.sems[0]).wait()
+            self.sent = True
+
     def send(src, dst, peer):
-        slot = len(started)
-        copy = pltpu.make_async_remote_copy(
-            src_ref=src, dst_ref=dst, send_sem=send_sem.at[slot], recv_sem=recv_sem.at[slot],
-            device_id=peer, device_id_type=MESH,
-        )
-        copy.start()
-        started.append(copy)
-        return copy
+        return Group(dst, [(src, dst, peer)])
+
+    def along_y(src, dst, size):
+        return Group(size, [(src(k), dst(k), y_peer[k]) for k in y_order])
+
+    def along_z(src, dst, size):
+        return Group(size, [(src(k), dst(k), z_peer[k]) for k in z_order])
 
     def store(src, dst):
         copy = pltpu.make_async_copy(src, dst, local_sem.at[len(loads) + len(stores)])
@@ -91,25 +110,24 @@
     y_order = (2, 1, 3)
 
     def gather(ref, c):
-        copies = [send(ref.at[xh, y, c, z], ref.at[xh, y, c, z], z_peer[k]) for k in z_order]
-        yield
-        for copy in copies:
-            copy.wait_recv()
-        along = ref.at[xh, y, c, :, :, high]
-        copies = [send(along, along, x_peer)]
-        along = ref.at[xh, y, c, :, :, low]
-        copies += [send(along, along, y_peer[k]) for k in y_order]
-        yield
-        for copy in copies[1:]:
-            copy.wait_recv()
-        along = ref.at[xh, :, c, :, :, low]
-        last = [send(along, along, x_peer)]
-        copies[0].wait_recv()
-        along = ref.at[:, y, c, :, :, high]
-        last += [send(along, along, y_peer[k]) for k in y_order]
-        yield
-        for copy in last:
-            copy.wait_recv()
+        own = ref.at[xh, y, c, z]
+        group = along_z(lambda k: own, lambda k: own, ref.at[xh, y, c, pl.ds(0, 7)])
+        yield
+        group.wait_recv()
+        own_high = ref.at[xh, y, c, :, :, high]
+        own_low = ref.at[xh, y, c, :, :, low]
+        over_y = along_y(lambda k: own_low, lambda k: own_low, ref.at[xh, pl.ds(0, 3), c, :, :, low])
+        over_x = send(own_high, own_high, x_peer)
+        yield
+        over_y.wait_recv()
+        all_low = ref.at[xh, :, c, :, :, low]
+        last_x = send(all_low, all_low, x_peer)
+        over_x.wait_recv()
+        both_high = ref.at[:, y, c, :, :, high]
+        last_y = along_y(lambda k: both_high, lambda k: both_high, ref.at[:, pl.ds(0, 3), c, :, :, high])
+        yield
+        last_x.wait_recv()
+        last_y.wait_recv()
 
     def turn(ref, c, stage, blocks):
         for j in blocks:
@@ -157,22 +175,19 @@
                 proj_out[c, k] = part.astype(BF16)
 
     def chain(c):
-        copies = [send(proj_out.at[c, k], proj_in.at[c, k], y_peer[k]) for k in y_order]
-        yield
-        for copy in copies:
-            copy.wait_recv()
+        group = along_y(lambda k: proj_out.at[c, k], lambda k: proj_in.at[c, k], proj_in.at[c, pl.ds(1, 3)])
+        yield
+        group.wait_recv()
         summed = proj_acc[c]
         for k in range(1, 4):
             summed = summed + proj_in[c, k].astype(F32)
         proj_acc[c] = summed
         fold_out[c] = summed.astype(BF16)
-        copies = [send(fold_out.at[c, z_at[k]], fold_in.at[c, k], z_peer[k]) for k in z_order]
+        group = along_z(lambda k: fold_out.at[c, z_at[k]], lambda k: fold_in.at[c, k], fold_in.at[c, pl.ds(1, 7)])
         yield
         if c == 0:
-            for copy in res_copies:
-                copy.wait_recv()
-        for copy in copies:
-            copy.wait_recv()
+            res_group.wait_recv()
+        group.wait_recv()
         own = proj_acc[c, z]
         for k in range(1, 8):
             own = own + fold_in[c, k].astype(F32)
@@ -194,18 +209,16 @@
         for at in range(NY):
             xa_out[c, at] = decode((1 - xh) * NY + at, low).astype(BF16)
         xa_copy = send(xa_out.at[c], xa_in.at[c], x_peer)
-        yb_copies = []
         for k in y_order:
             for m in range(NX):
                 yb_out[c, k, m] = decode(m * NY + y_at[k], high).astype(BF16)
-            yb_copies.append(send(yb_out.at[c, k], yb_in.at[c, k], y_peer[k]))
+        yb_group = along_y(lambda k: yb_out.at[c, k], lambda k: yb_in.at[c, k], yb_in.at[c, pl.ds(1, 3)])
         for at in range(NY):
             xa_own[c, at] = decode(xh * NY + at, low)
         for m in range(NX):
             yb_own[c, m] = decode(m * NY + y, high)
         yield
         xa_copy.wait_recv()
-        ya_copies = []
         for k in y_order + (0,):
             at = y_at[k]
             part = xa_own[c, at] + xa_in[c, at].astype(F32)
@@ -213,9 +226,8 @@
                 z_own[c, :, :, :HALF] = part
             else:
                 ya_out[c, k] = part.astype(BF16)
-                ya_copies.append(send(ya_out.at[c, k], ya_in.at[c, k], y_peer[k]))
-        for copy in yb_copies:
-            copy.wait_recv()
+        ya_group = along_y(lambda k: ya_out.at[c, k], lambda k: ya_in.at[c, k], ya_in.at[c, pl.ds(1, 3)])
+        yb_group.wait_recv()
 
         def over_y(m):
             part = yb_own[c, m]
@@ -227,8 +239,7 @@
         xb_copy = send(xb_out.at[c], xb_in.at[c], x_peer)
         z_own[c, :, :, HALF:] = over_y(xh)
         yield
-        for copy in ya_copies:
-            copy.wait_recv()
+        ya_group.wait_recv()
         part = z_own[c, :, :, :HALF]
         for k in range(1, 4):
             part = part + ya_in[c, k].astype(F32)
@@ -238,10 +249,9 @@
         part = z_own[c, :, :, HALF:] + xb_in[c].astype(F32)
         z_own[c, :, :, HALF:] = part
         z_out[c, :, :, HALF:] = part.astype(BF16)
-        copies = [send(z_out.at[c, z_at[k]], z_in.at[c, k], z_peer[k]) for k in z_order]
-        yield
-        for copy in copies:
-            copy.wait_recv()
+        group = along_z(lambda k: z_out.at[c, z_at[k]], lambda k: z_in.at[c, k], z_in.at[c, pl.ds(1, 7)])
+        yield
+        group.wait_recv()
         recon = z_own[c, z]
         for k in range(1, 8):
             recon = recon + z_in[c, k].astype(F32)
@@ -263,7 +273,7 @@
     pl.semaphore_wait(barrier, len(partners))
     first, second = chain(0), chain(1)
     next(first)
-    res_copies = [send(res_out.at[k], res_in.at[k], y_peer[k]) for k in y_order]
+    res_group = along_y(lambda k: res_out.at[k], lambda k: res_in.at[k], res_in.at[pl.ds(1, 3)])
     project(1)
     for _ in range(DELAY):
         next(first)
@@ -272,42 +282,32 @@
         for one in list(running):
             if next(one, "end") == "end":
                 running.remove(one)
-    for copy in started:
-        copy.wait_send()
+            for group in groups[:-LATE]:
+                group.wait_send()
+    for group in groups:
+        group.wait_send()
     for copy in stores:
         copy.wait()
 
 
-def gradient_kernel(
-    turned_hbm, feats_hbm, gpre_hbm, grad_hbm, bias_grad, turned, code, grad, code_sem, in_sem, out_sem
-):
-    first = [
-        pltpu.make_async_copy(gpre_hbm, code.at[0], code_sem.at[0]),
-        pltpu.make_async_copy(feats_hbm, code.at[1], code_sem.at[1]),
-    ]
-    blocks = [
-        pltpu.make_async_copy(turned_hbm.at[:, :, j], turned.at[:, :, j], in_sem.at[j]) for j in range(NX * NY)
-    ]
-    for copy in first + blocks:
-        copy.start()
-    for copy in first:
-        copy.wait()
-    right = code[...].reshape(4 * CHUNK, LAT)
+def gradient_kernel(turned, feats, gpre, grad_hbm, bias_grad, grad, out_sem):
+    slope = gpre[...].reshape(2 * CHUNK, LAT)
+    right = jnp.concatenate([slope, feats[...].reshape(2 * CHUNK, LAT)], axis=0)
     stores = []
     for j in range(NX * NY):
-        blocks[j].wait()
         left = jnp.concatenate([turned[s, c, j] for s in range(2) for c in range(2)], axis=1)
         grad[j] = jnp.dot(left, right, preferred_element_type=F32).astype(BF16)
         copy = pltpu.make_async_copy(grad.at[j], grad_hbm.at[j], out_sem.at[j])
         copy.start()
         stores.append(copy)
-    bias_grad[...] = jnp.sum(code[0].astype(F32).reshape(2 * CHUNK, LAT), axis=0, keepdims=True)
+    bias_grad[...] = jnp.sum(slope.astype(F32), axis=0, keepdims=True)
     for copy in stores:
         copy.wait()
 
 
 def body(attention, out_proj, residual, dictionary, enc_bias, active):
     hbm = pl.BlockSpec(memory_space=pl.ANY)
+    vmem = pl.BlockSpec(memory_space=pltpu.VMEM)
     piece = (NX, NY, 2, NZ, ROWS, FEAT)
     code = (2, NZ, ROWS, LAT)
     half = (NZ, ROWS, HALF)
@@ -315,8 +315,8 @@
     shapes = [flipped, code, code]
     turned, feats, gpre = pl.pallas_call(
         step_kernel,
-        out_shape=[jax.ShapeDtypeStruct(s, BF16) for s in shapes],
-        in_specs=[hbm] * 6,
+        out_shape=[pltpu.VMEM(s, BF16) for s in shapes],
+        in_specs=[pl.BlockSpec(memory_space=pltpu.HBM)] * 6,
         out_specs=[hbm] * 3,
         scratch_shapes=[
             pltpu.VMEM(flipped, BF16),
@@ -360,7 +360,7 @@
             pltpu.SemaphoreType.DMA((SENDS,)),
         ],
         compiler_params=pltpu.CompilerParams(
-            collective_id=0, has_side_effects=True, vmem_limit_bytes=60 << 20
+            collective_id=0, has_side_effects=True, vmem_limit_bytes=50 << 20
         ),
         name="crosscoder_step",
     )(
@@ -377,17 +377,13 @@
             jax.ShapeDtypeStruct((NX * NY, FEAT, LAT), BF16),
             jax.ShapeDtypeStruct((1, LAT), F32),
         ],
-        in_specs=[hbm] * 3,
-        out_specs=[hbm, pl.BlockSpec(memory_space=pltpu.VMEM)],
+        in_specs=[vmem] * 3,
+        out_specs=[hbm, vmem],
         scratch_shapes=[
-            pltpu.VMEM(flipped, BF16),
-            pltpu.VMEM((2,) + code, BF16),
             pltpu.VMEM((NX * NY, FEAT, LAT), BF16),
-            pltpu.SemaphoreType.DMA((2,)),
-            pltpu.SemaphoreType.DMA((NX * NY,)),
             pltpu.SemaphoreType.DMA((NX * NY,)),
         ],
-        compiler_params=pltpu.CompilerParams(vmem_limit_bytes=60 << 20),
+        compiler_params=pltpu.CompilerParams(vmem_limit_bytes=24 << 20),
         name="dictionary_gradient",
     )(turned, feats, gpre)
     return grad.reshape(dictionary.shape), bias_grad.reshape(LAT)

time: 117 us -> 112 us (0.957)
  Pallas kernels: 116 us -> 111 us
    pallas_call x1, Pallas kernels: 7.2 us -> 3.8 us  [body(): pl.pallas_call(gradient_kernel, out_shape=[jax.ShapeDtypeStruct((NX * NY,...]
    pallas_call x1, Pallas kernels: 109 us -> 107 us  [body(): pl.pallas_call(step_kernel, out_shape=[pltpu.VMEM(s, BF16) for s in shape...]
where the time goes in v3:
time: 112 us; the launch traced here: 111 us
  Pallas kernels  111 us (99%)
    pallas_call x1, Pallas kernels, body(): pl.pallas_call(step_kernel, out_shape=[pltpu.VMEM(s, BF16) for s in shape...  107 us
    pallas_call x1, Pallas kernels, body(): pl.pallas_call(gradient_kernel, out_shape=[jax.ShapeDtypeStruct((NX * NY,...  3.8 us

profile of v3, /device:TPU:1, one launch (start us, length us, event | category | flops | bytes accessed | tf_op | source)
XLA Modules:
  0.0 111.4 jit_solution(17626254215909137765)
XLA Ops:
  0.6 107.0 %crosscoder_step.1 = (bf16[2,2,8,512,128]{4,3,2,1,0:T(8,128)(2,1)S(1)}, bf16[2,8,16,512]{3,2,1,0:T(8,128)(2,1)S(1)}, bf16[2,8,16,512]{3,2,1,0:T(8,128)(2,1)S(1)}) custom-call(bf16[8,2,16,256]{3,2,1,0:T(8,128)(2,1)} %bitcast.8, bf16[256,2048]{1,0:T(8,128)(2,1)} %proj_hbm.1, bf16[8,2048]{1,0:T(8,128)(2,1)} %resid_hbm.1, bf16[8,512,512]{2,1,0:T(8,128)(2,1)} %bitcast.6, ...), custom_call_target="tpu_custom_call" | custom-call | tf_op jit(solution)/shard_map/crosscoder_step/pallas_call | solution.py:316
  107.6 3.8 %dictionary_gradient.1 = (bf16[8,512,512]{2,1,0:T(8,128)(2,1)}, f32[1,512]{1,0:T(1,128)}) custom-call(bf16[2,2,8,512,128]{4,3,2,1,0:T(8,128)(2,1)S(1)} %get-tuple-element.7.turned, bf16[2,8,16,512]{3,2,1,0:T(8,128)(2,1)S(1)} %get-tuple-element.8.feats, bf16[2,8,16,512]{3,2,1,0:T(8,128)(2,1)S(1)} %get-tuple-element.9.gpre), custom_call_target="tpu_custom_call" | custom-call | tf_op jit(solution)/shard_map/dictionary_gradient/pallas_call | solution.py:374

commit v4 on v3

--- a/solution.py
+++ b/solution.py
@@ -14,9 +14,8 @@
 FEAT = 512
 LAT = 512
 SENDS = 47
-LATE = 46
 HALF = 256
-DELAY = 1
+ORDER = "01010001100110011001101101010011100110011"
 
 
 def nt_dot(left, right):
@@ -122,6 +121,7 @@
         over_y.wait_recv()
         all_low = ref.at[xh, :, c, :, :, low]
         last_x = send(all_low, all_low, x_peer)
+        yield
         over_x.wait_recv()
         both_high = ref.at[:, y, c, :, :, high]
         last_y = along_y(lambda k: both_high, lambda k: both_high, ref.at[:, pl.ds(0, 3), c, :, :, high])
@@ -227,6 +227,7 @@
             else:
                 ya_out[c, k] = part.astype(BF16)
         ya_group = along_y(lambda k: ya_out.at[c, k], lambda k: ya_in.at[c, k], ya_in.at[c, pl.ds(1, 3)])
+        yield
         yb_group.wait_recv()
 
         def over_y(m):
@@ -275,15 +276,11 @@
     next(first)
     res_group = along_y(lambda k: res_out.at[k], lambda k: res_in.at[k], res_in.at[pl.ds(1, 3)])
     project(1)
-    for _ in range(DELAY):
-        next(first)
-    running = [second, first]
-    while running:
-        for one in list(running):
-            if next(one, "end") == "end":
-                running.remove(one)
-            for group in groups[:-LATE]:
+    for turn_at, turn_of in enumerate(ORDER):
+        if turn_at == len(ORDER) - 4:
+            for group in groups[:-12]:
                 group.wait_send()
+        next((first, second)[int(turn_of)], None)
     for group in groups:
         group.wait_send()
     for copy in stores:

time: 112 us -> 108 us (0.964)
  Pallas kernels: 111 us -> 106 us
    pallas_call x1, Pallas kernels: 107 us -> 103 us  [body(): pl.pallas_call(step_kernel, out_shape=[pltpu.VMEM(s, BF16) for s in shape...]
where the time goes in v4:
time: 108 us; the launch traced here: 107 us
  Pallas kernels  106 us (98%)
    pallas_call x1, Pallas kernels, body(): pl.pallas_call(step_kernel, out_shape=[pltpu.VMEM(s, BF16) for s in shape...  103 us
    pallas_call x1, Pallas kernels, body(): pl.pallas_call(gradient_kernel, out_shape=[jax.ShapeDtypeStruct((NX * NY,...  3.8 us

profile of v4, /device:TPU:1, one launch (start us, length us, event | category | flops | bytes accessed | tf_op | source)
XLA Modules:
  0.0 107.0 jit_solution(7273983702043148269)
XLA Ops:
  0.6 102.5 %crosscoder_step.1 = (bf16[2,2,8,512,128]{4,3,2,1,0:T(8,128)(2,1)S(1)}, bf16[2,8,16,512]{3,2,1,0:T(8,128)(2,1)S(1)}, bf16[2,8,16,512]{3,2,1,0:T(8,128)(2,1)S(1)}) custom-call(bf16[8,2,16,256]{3,2,1,0:T(8,128)(2,1)} %bitcast.8, bf16[256,2048]{1,0:T(8,128)(2,1)} %proj_hbm.1, bf16[8,2048]{1,0:T(8,128)(2,1)} %resid_hbm.1, bf16[8,512,512]{2,1,0:T(8,128)(2,1)} %bitcast.6, ...), custom_call_target="tpu_custom_call" | custom-call | tf_op jit(solution)/shard_map/crosscoder_step/pallas_call | solution.py:313
  103.2 3.8 %dictionary_gradient.1 = (bf16[8,512,512]{2,1,0:T(8,128)(2,1)}, f32[1,512]{1,0:T(1,128)}) custom-call(bf16[2,2,8,512,128]{4,3,2,1,0:T(8,128)(2,1)S(1)} %get-tuple-element.7.turned, bf16[2,8,16,512]{3,2,1,0:T(8,128)(2,1)S(1)} %get-tuple-element.8.feats, bf16[2,8,16,512]{3,2,1,0:T(8,128)(2,1)S(1)} %get-tuple-element.9.gpre), custom_call_target="tpu_custom_call" | custom-call | tf_op jit(solution)/shard_map/dictionary_gradient/pallas_call | solution.py:371

commit v5 on v4

v5 whole, which is shorter than its diff:
```python
import jax
import jax.numpy as jnp
from jax import lax
from jax.experimental import pallas as pl
from jax.experimental.pallas import tpu as pltpu
from jax.sharding import PartitionSpec as P

MESH = pl.DeviceIdType.MESH
F32 = jnp.float32
BF16 = jnp.bfloat16
NX, NZ, NY = 2, 4, 4
NC = 4
ROWS = 16
CHUNK = NZ * ROWS
FEAT = 512
LAT = 512
SENDS = 93
HALF = 256
ORDER = ("10120312031002311020122031013321200321032", "310312233102310023110213221330123230232013")


def nt_dot(left, right):
    return lax.dot_general(left, right, (((1,), (1,)), ((), ())), preferred_element_type=F32)


def tn_dot(left, right):
    return lax.dot_general(left, right, (((0,), (0,)), ((), ())), preferred_element_type=F32)


def step_kernel(
    attn_hbm, proj_hbm, resid_hbm, dict_hbm, bias_hbm, act_hbm,
    turned_hbm, feats_hbm, gpre_hbm,
    turned, attn, proj, resid, dic, bias, act, fields, errors, feats, gpre,
    res_out, res_in,
    proj_acc, proj_out, proj_in, fold_out, fold_in,
    pre, half_out, half_in, pair_out, pair_in,
    xa_out, xa_in, xa_own, ya_out, ya_in,
    yb_out, yb_in, yb_own, xb_out, xb_in,
    z_own, z_out, z_in,
    local_sem, send_sem, recv_sem,
):
    wide = lax.axis_index("wide")
    narrow = lax.axis_index("narrow")
    xh, z, y = wide // 32, (wide // 4) % 8, wide % 4
    zh, zl = z // 2, z % 2
    xl, core = narrow // 2, narrow % 2

    def dev(xh_=xh, z_=z, y_=y, xl_=xl, core_=core):
        return ((xh_ * 8 + z_) * 4 + y_, xl_ * 2 + core_)

    x_peer = dev(xh_=1 - xh)
    pair_peer = dev(xl_=1 - xl)
    core_peer = dev(core_=1 - core)
    y_at = [(y + k) % 4 for k in range(4)]
    z_at = [(z + k) % 8 for k in range(8)]
    y_peer = [dev(y_=at) for at in y_at]
    z_peer = [dev(z_=at) for at in z_at]
    across = [dev(z_=z + 1 - 2 * zl, y_=at) for at in y_at]

    barrier = pltpu.get_barrier_semaphore()
    partners = [x_peer, pair_peer, core_peer] + y_peer[1:] + z_peer[1:] + across[1:]
    for peer in partners:
        pl.semaphore_signal(barrier, inc=1, device_id=peer, device_id_type=MESH)

    loads = []
    for src, dst in (
        (attn_hbm, attn), (proj_hbm, proj), (resid_hbm, resid),
        (bias_hbm, bias), (act_hbm, act), (dict_hbm, dic),
    ):
        copy = pltpu.make_async_copy(src, dst, local_sem.at[len(loads)])
        copy.start()
        loads.append(copy)

    groups = []
    stores = []

    class Group:
        def __init__(self, size, copies):
            slot = len(groups)
            self.size, self.sems, self.sent = size, (send_sem.at[slot], recv_sem.at[slot]), False
            for src, dst, peer in copies:
                pltpu.make_async_remote_copy(
                    src_ref=src, dst_ref=dst, send_sem=self.sems[0], recv_sem=self.sems[1],
                    device_id=peer, device_id_type=MESH,
                ).start()
            groups.append(self)

        def wait_recv(self):
            pltpu.make_async_copy(self.size, self.size, self.sems[1]).wait()

        def wait_send(self):
            if not self.sent:
                pltpu.make_async_copy(self.size, self.size, self.sems[0]).wait()
            self.sent = True

    def send(src, dst, peer):
        return Group(dst, [(src, dst, peer)])

    def along_y(src, dst, size):
        return Group(size, [(src(k), dst(k), y_peer[k]) for k in y_order])

    def along_z(src, dst, size):
        return Group(size, [(src(k), dst(k), z_peer[k]) for k in z_order])

    def store(src, dst):
        copy = pltpu.make_async_copy(src, dst, local_sem.at[len(loads) + len(stores)])
        copy.start()
        stores.append(copy)

    halves = (pl.ds(0, HALF), pl.ds(HALF, HALF))
    z_order = (4, 3, 5, 2, 6, 1, 7)
    y_order = (2, 1, 3)

    def gather(ref, c):
        own = ref.at[xh, y, zl, c, zh]
        group = along_z(lambda k: own, lambda k: own, fold_in.at[c, pl.ds(1, 7)])
        yield
        group.wait_recv()
        own_low, own_high = ref.at[xh, y, 0, c], ref.at[xh, y, 1, c]
        over_y = along_y(lambda k: own_low, lambda k: own_low, ref.at[xh, pl.ds(0, 3), 0, c])
        over_x = send(own_high, own_high, x_peer)
        yield
        over_y.wait_recv()
        all_low = ref.at[xh, :, 0, c]
        last_x = send(all_low, all_low, x_peer)
        yield
        over_x.wait_recv()
        both_high = ref.at[:, y, 1, c]
        last_y = along_y(lambda k: both_high, lambda k: both_high, ref.at[:, pl.ds(0, 3), 1, c])
        yield
        last_x.wait_recv()
        last_y.wait_recv()

    gathered = {}
    seen = []

    def once(name):
        seen.append(name)
        return seen.count(name) == 1

    def turn(ref, pair, stage, blocks):
        for j in blocks:
            for h in range(2):
                rows = ref[j // NY, j % NY, h, pl.ds(2 * pair, 2)].reshape(2 * CHUNK, HALF)
                turned[stage, pair, j, halves[h], :] = rows.T

    def encode(ref, c, result, stage, with_bias):
        gathered[stage, c // 2] = gathered.get((stage, c // 2), 0) + 1
        both = gathered[stage, c // 2] == 2
        total = None
        for m in range(NX):
            for at in range(NY):
                for h in range(2):
                    rows = ref[m, at, h, c].reshape(CHUNK, HALF)
                    part = jnp.dot(rows, dic[m * NY + at, halves[h], :], preferred_element_type=F32)
                    total = part if total is None else total + part
        pre[c, stage] = total
        mine = pl.ds(pl.multiple_of(core * 32, 32), 32)
        theirs = pl.ds(pl.multiple_of((1 - core) * 32, 32), 32)
        half_out[c, stage] = pre[c, stage, theirs, :].astype(BF16)
        copy = send(half_out.at[c, stage], half_in.at[c, stage], core_peer)
        if both:
            turn(ref, c // 2, stage, (0, 1))
        yield
        copy.wait_recv()
        half = (pre[c, stage, mine, :] + half_in[c, stage].astype(F32)).astype(BF16)
        pair_out[c, stage] = half
        copy = send(pair_out.at[c, stage], pair_in.at[c, stage], pair_peer)
        if both:
            turn(ref, c // 2, stage, range(2, NX * NY))
            store(turned.at[stage, c // 2], turned_hbm.at[stage, c // 2])
        yield
        copy.wait_recv()
        total = pair_out[c, stage].astype(F32) + pair_in[c, stage].astype(F32)
        if with_bias:
            total = total + bias[...]
        places = pl.ds(core * 2, 2)
        mask = act[places, c].reshape(32, LAT).astype(F32)
        result[c, places] = (mask * total).astype(BF16).reshape(2, ROWS, LAT)
        copy = send(result.at[c, places], result.at[c, places], core_peer)
        yield
        copy.wait_recv()

    def project(c):
        rows = attn[:, c].reshape(CHUNK, 256)
        for k in y_order + (0,):
            cols = pl.ds(pl.multiple_of(y_at[k] * FEAT, FEAT), FEAT)
            part = jnp.dot(rows, proj[:, cols], preferred_element_type=F32)
            for h in range(2):
                half = part[:, h * HALF:(h + 1) * HALF].reshape(NZ, ROWS, HALF)
                if k == 0:
                    proj_acc[c, h] = half
                else:
                    proj_out[c, k, h] = half.astype(BF16)

    def chain(c):
        group = along_y(lambda k: proj_out.at[c, k], lambda k: proj_in.at[c, k], proj_in.at[c, pl.ds(1, 3)])
        yield
        group.wait_recv()
        summed = proj_acc[c]
        for k in range(1, 4):
            summed = summed + proj_in[c, k].astype(F32)
        proj_acc[c] = summed
        fold_out[c] = summed.astype(BF16)
        group = along_z(lambda k: fold_out.at[c, z_at[k] % 2, z_at[k] // 2], lambda k: fold_in.at[c, k], fold_in.at[c, pl.ds(1, 7)])
        yield
        if once("residual"):
            res_group.wait_recv()
        group.wait_recv()
        own = proj_acc[c, zl, zh]
        for k in range(1, 8):
            own = own + fold_in[c, k].astype(F32)
        from_half = 4 * ((zl + c // 2) % 2)
        upper = res_in[from_half + (y - 2 * (c % 2) + 4) % 4]
        lower = res_in[from_half + (y - 2 * (c % 2) + 3) % 4]
        fields[xh, y, zl, c, zh] = (own + jnp.concatenate([upper, lower], axis=0)).astype(BF16)
        yield from gather(fields, c)
        if once("loads"):
            for copy in loads[3:]:
                copy.wait()
        yield from encode(fields, c, feats, 0, True)
        store(feats.at[c], feats_hbm.at[c])

        code = feats[c].reshape(CHUNK, LAT)

        def decode(j, h):
            return nt_dot(code, dic[j, halves[h], :]).reshape(NZ, ROWS, HALF)

        for at in range(NY):
            xa_out[c, at] = decode((1 - xh) * NY + at, 0).astype(BF16)
        xa_copy = send(xa_out.at[c], xa_in.at[c], x_peer)
        for k in y_order:
            for m in range(NX):
                yb_out[c, k, m] = decode(m * NY + y_at[k], 1).astype(BF16)
        yb_group = along_y(lambda k: yb_out.at[c, k], lambda k: yb_in.at[c, k], yb_in.at[c, pl.ds(1, 3)])
        for at in range(NY):
            xa_own[c, at] = decode(xh * NY + at, 0)
        for m in range(NX):
            yb_own[c, m] = decode(m * NY + y, 1)
        yield
        xa_copy.wait_recv()
        for k in y_order + (0,):
            at = y_at[k]
            part = xa_own[c, at] + xa_in[c, at].astype(F32)
            if k == 0:
                z_own[c, 0] = part
            else:
                ya_out[c, k] = part.astype(BF16)
        ya_group = along_y(lambda k: ya_out.at[c, k], lambda k: ya_in.at[c, k], ya_in.at[c, pl.ds(1, 3)])
        yield
        yb_group.wait_recv()

        def over_y(m):
            part = yb_own[c, m]
            for k in range(1, 4):
                part = part + yb_in[c, k, m].astype(F32)
            return part

        xb_out[c] = over_y(1 - xh).astype(BF16)
        xb_copy = send(xb_out.at[c], xb_in.at[c], x_peer)
        z_own[c, 1] = over_y(xh)
        yield
        ya_group.wait_recv()
        part = z_own[c, 0]
        for k in range(1, 4):
            part = part + ya_in[c, k].astype(F32)
        z_own[c, 0] = part
        z_out[c, 0] = part.astype(BF16)
        xb_copy.wait_recv()
        part = z_own[c, 1] + xb_in[c].astype(F32)
        z_own[c, 1] = part
        z_out[c, 1] = part.astype(BF16)
        group = along_z(lambda k: z_out.at[c, z_at[k] % 2, z_at[k] // 2], lambda k: z_in.at[c, k], z_in.at[c, pl.ds(1, 7)])
        yield
        group.wait_recv()
        recon = z_own[c, zl, zh]
        for k in range(1, 8):
            recon = recon + z_in[c, k].astype(F32)
        errors[xh, y, zl, c, zh] = (recon - fields[xh, y, zl, c, zh].astype(F32)).astype(BF16)
        yield from gather(errors, c)
        yield from encode(errors, c, gpre, 1, False)
        store(gpre.at[c], gpre_hbm.at[c])

    for copy in loads[:2]:
        copy.wait()
    project(0)
    loads[2].wait()
    for d in range(2):
        for k in range(4):
            start = y_at[k] * FEAT + ((zl + d) % 2) * HALF
            rows = resid[:, pl.ds(pl.multiple_of(start, HALF), HALF)].astype(F32)
            if d == 0 and k == 0:
                res_in[0] = rows
            else:
                res_out[4 * d + k] = rows
    pl.semaphore_wait(barrier, len(partners))
    chains = [chain(c) for c in range(NC)]
    next(chains[0])
    res_copies = [(res_out.at[k], res_in.at[k], y_peer[k]) for k in y_order]
    res_copies += [(res_out.at[4 + k], res_in.at[4 + k], across[k]) for k in (2, 1, 3, 0)]
    res_group = Group(res_in.at[pl.ds(1, 7)], res_copies)
    for c in range(1, NC):
        project(c)
    for turn_at, turn_of in enumerate(ORDER[0] + ORDER[1]):
        if turn_at == 3 * 21 + 20 - 6:
            for group in groups[:-20]:
                group.wait_send()
        next(chains[int(turn_of)], None)
    for group in groups:
        group.wait_send()
    for copy in stores:
        copy.wait()


def gradient_kernel(turned, feats, gpre, grad_hbm, bias_grad, grad, out_sem):
    slope = gpre[...].reshape(NC * CHUNK, LAT)
    right = jnp.concatenate([slope, feats[...].reshape(NC * CHUNK, LAT)], axis=0)
    stores = []
    for j in range(NX * NY):
        left = jnp.concatenate([turned[s, c, j] for s in range(2) for c in range(2)], axis=1)
        grad[j] = jnp.dot(left, right, preferred_element_type=F32).astype(BF16)
        copy = pltpu.make_async_copy(grad.at[j], grad_hbm.at[j], out_sem.at[j])
        copy.start()
        stores.append(copy)
    bias_grad[...] = jnp.sum(slope.astype(F32), axis=0, keepdims=True)
    for copy in stores:
        copy.wait()


def body(attention, out_proj, residual, dictionary, enc_bias, active):
    hbm = pl.BlockSpec(memory_space=pl.ANY)
    vmem = pl.BlockSpec(memory_space=pltpu.VMEM)
    half = (NZ, ROWS, HALF)
    piece = (NX, NY, 2, NC) + half
    code = (NC, NZ, ROWS, LAT)
    flipped = (2, 2, NX * NY, FEAT, 2 * CHUNK)
    narrow_half = (NC, 2, 32, LAT)
    shapes = [flipped, code, code]
    turned, feats, gpre = pl.pallas_call(
        step_kernel,
        out_shape=[pltpu.VMEM(s, BF16) for s in shapes],
        in_specs=[pl.BlockSpec(memory_space=pltpu.HBM)] * 6,
        out_specs=[hbm] * 3,
        scratch_shapes=[
            pltpu.VMEM(flipped, BF16),
            pltpu.VMEM((NZ, NC, ROWS, 256), BF16),
            pltpu.VMEM((256, NY * FEAT), BF16),
            pltpu.VMEM((8, NY * FEAT), BF16),
            pltpu.VMEM((NX * NY, FEAT, LAT), BF16),
            pltpu.VMEM((1, LAT), F32),
            pltpu.VMEM((NZ, NC, ROWS, LAT), jnp.int32),
            pltpu.VMEM(piece, BF16),
            pltpu.VMEM(piece, BF16),
            pltpu.VMEM(code, BF16),
            pltpu.VMEM(code, BF16),
            pltpu.VMEM((8, 8, HALF), F32),
            pltpu.VMEM((8, 8, HALF), F32),
            pltpu.VMEM((NC, 2) + half, F32),
            pltpu.VMEM((NC, 4, 2) + half, BF16),
            pltpu.VMEM((NC, 4, 2) + half, BF16),
            pltpu.VMEM((NC, 2) + half, BF16),
            pltpu.VMEM((NC, 8, ROWS, HALF), BF16),
            pltpu.VMEM((NC, 2, CHUNK, LAT), F32),
            pltpu.VMEM(narrow_half, BF16),
            pltpu.VMEM(narrow_half, BF16),
            pltpu.VMEM(narrow_half, BF16),
            pltpu.VMEM(narrow_half, BF16),
            pltpu.VMEM((NC, NY) + half, BF16),
            pltpu.VMEM((NC, NY) + half, BF16),
            pltpu.VMEM((NC, NY) + half, F32),
            pltpu.VMEM((NC, 4) + half, BF16),
            pltpu.VMEM((NC, 4) + half, BF16),
            pltpu.VMEM((NC, 4, NX) + half, BF16),
            pltpu.VMEM((NC, 4, NX) + half, BF16),
            pltpu.VMEM((NC, NX) + half, F32),
            pltpu.VMEM((NC,) + half, BF16),
            pltpu.VMEM((NC,) + half, BF16),
            pltpu.VMEM((NC, 2) + half, F32),
            pltpu.VMEM((NC, 2) + half, BF16),
            pltpu.VMEM((NC, 8, ROWS, HALF), BF16),
            pltpu.SemaphoreType.DMA((18,)),
            pltpu.SemaphoreType.DMA((SENDS,)),
            pltpu.SemaphoreType.DMA((SENDS,)),
        ],
        compiler_params=pltpu.CompilerParams(
            collective_id=0, has_side_effects=True, vmem_limit_bytes=50 << 20
        ),
        name="crosscoder_step",
    )(
        attention.reshape(NZ, NC, ROWS, 256),
        out_proj,
        residual,
        dictionary.reshape(NX * NY, FEAT, LAT),
        enc_bias.reshape(1, LAT),
        active.reshape(NZ, NC, ROWS, LAT),
    )
    grad, bias_grad = pl.pallas_call(
        gradient_kernel,
        out_shape=[
            jax.ShapeDtypeStruct((NX * NY, FEAT, LAT), BF16),
            jax.ShapeDtypeStruct((1, LAT), F32),
        ],
        in_specs=[vmem] * 3,
        out_specs=[hbm, vmem],
        scratch_shapes=[
            pltpu.VMEM((NX * NY, FEAT, LAT), BF16),
            pltpu.SemaphoreType.DMA((NX * NY,)),
        ],
        compiler_params=pltpu.CompilerParams(vmem_limit_bytes=24 << 20),
        name="dictionary_gradient",
    )(turned, feats, gpre)
    return grad.reshape(dictionary.shape), bias_grad.reshape(LAT)


def solution(mesh):
    in_specs = (
        P(None, "wide"),
        P("wide", "narrow"),
        P("wide", "narrow"),
        P(None, "narrow", "wide"),
        P("wide"),
        P(None, "wide"),
    )
    out_specs = (P(None, "narrow", "wide"), P("wide"))
    return jax.shard_map(body, mesh=mesh, in_specs=in_specs, out_specs=out_specs, check_vma=False)
```

time: 108 us -> 106 us (0.981)
    pallas_call x1, Pallas kernels: 103 us -> 101 us  [body(): pl.pallas_call(step_kernel, out_shape=[pltpu.VMEM(s, BF16) for s in shape...]
where the time goes in v5:
time: 106 us
  Pallas kernels  105 us (99%)
    pallas_call x1, Pallas kernels, body(): pl.pallas_call(step_kernel, out_shape=[pltpu.VMEM(s, BF16) for s in shape...  101 us
    pallas_call x1, Pallas kernels, body(): pl.pallas_call(gradient_kernel, out_shape=[jax.ShapeDtypeStruct((NX * NY,...  3.8 us

profile of v5, /device:TPU:1, one launch (start us, length us, event | category | flops | bytes accessed | tf_op | source)
XLA Modules:
  0.0 106.1 jit_solution(5024775550137129442)
XLA Ops:
  0.6 101.5 %crosscoder_step.1 = (bf16[2,2,8,512,128]{4,3,2,1,0:T(8,128)(2,1)S(1)}, bf16[4,4,16,512]{3,2,1,0:T(8,128)(2,1)S(1)}, bf16[4,4,16,512]{3,2,1,0:T(8,128)(2,1)S(1)}) custom-call(bf16[4,4,16,256]{3,2,1,0:T(8,128)(2,1)} %bitcast.8, bf16[256,2048]{1,0:T(8,128)(2,1)} %proj_hbm.1, bf16[8,2048]{1,0:T(8,128)(2,1)} %resid_hbm.1, bf16[8,512,512]{2,1,0:T(8,128)(2,1)} %bitcast.6, ...), custom_call_target="tpu_custom_call" | custom-call | tf_op jit(solution)/shard_map/crosscoder_step/pallas_call | solution.py:339
  102.1 3.8 %dictionary_gradient.1 = (bf16[8,512,512]{2,1,0:T(8,128)(2,1)}, f32[1,512]{1,0:T(1,128)}) custom-call(bf16[2,2,8,512,128]{4,3,2,1,0:T(8,128)(2,1)S(1)} %get-tuple-element.7.turned, bf16[4,4,16,512]{3,2,1,0:T(8,128)(2,1)S(1)} %get-tuple-element.8.feats, bf16[4,4,16,512]{3,2,1,0:T(8,128)(2,1)S(1)} %get-tuple-element.9.gpre), custom_call_target="tpu_custom_call" | custom-call | tf_op jit(solution)/shard_map/dictionary_gradient/pallas_call | solution.py:397

commit v6 on v5

--- a/solution.py
+++ b/solution.py
@@ -16,7 +16,7 @@
 LAT = 512
 SENDS = 93
 HALF = 256
-ORDER = ("10120312031002311020122031013321200321032", "310312233102310023110213221330123230232013")
+ORDER = ("10321012031002311020122013023321001203231", "013223102331020312311022031133223032103123")
 
 
 def nt_dot(left, right):
@@ -177,7 +177,11 @@
         places = pl.ds(core * 2, 2)
         mask = act[places, c].reshape(32, LAT).astype(F32)
         result[c, places] = (mask * total).astype(BF16).reshape(2, ROWS, LAT)
-        copy = send(result.at[c, places], result.at[c, places], core_peer)
+        place = result.at[c, places]
+        if stage:
+            place = gpre_hbm.at[c, places]
+            store(result.at[c, places], place)
+        copy = send(result.at[c, places], place, core_peer)
         yield
         copy.wait_recv()
 
@@ -279,7 +283,6 @@
         errors[xh, y, zl, c, zh] = (recon - fields[xh, y, zl, c, zh].astype(F32)).astype(BF16)
         yield from gather(errors, c)
         yield from encode(errors, c, gpre, 1, False)
-        store(gpre.at[c], gpre_hbm.at[c])
 
     for copy in loads[:2]:
         copy.wait()

time: 106 us -> 105 us (level)
  no operation moved by 1% of the time
where the time goes in v6:
time: 105 us
  Pallas kernels  104 us (99%)
    pallas_call x1, Pallas kernels, body(): pl.pallas_call(step_kernel, out_shape=[pltpu.VMEM(s, BF16) for s in shape...  101 us
    pallas_call x1, Pallas kernels, body(): pl.pallas_call(gradient_kernel, out_shape=[jax.ShapeDtypeStruct((NX * NY,...  3.8 us

profile of v6, /device:TPU:1, one launch (start us, length us, event | category | flops | bytes accessed | tf_op | source)
XLA Modules:
  0.0 105.2 jit_solution(9948296615398896395)
XLA Ops:
  0.6 100.6 %crosscoder_step.1 = (bf16[2,2,8,512,128]{4,3,2,1,0:T(8,128)(2,1)S(1)}, bf16[4,4,16,512]{3,2,1,0:T(8,128)(2,1)S(1)}, bf16[4,4,16,512]{3,2,1,0:T(8,128)(2,1)S(1)}) custom-call(bf16[4,4,16,256]{3,2,1,0:T(8,128)(2,1)} %bitcast.8, bf16[256,2048]{1,0:T(8,128)(2,1)} %proj_hbm.1, bf16[8,2048]{1,0:T(8,128)(2,1)} %resid_hbm.1, bf16[8,512,512]{2,1,0:T(8,128)(2,1)} %bitcast.6, ...), custom_call_target="tpu_custom_call" | custom-call | tf_op jit(solution)/shard_map/crosscoder_step/pallas_call | solution.py:342
  101.3 3.8 %dictionary_gradient.1 = (bf16[8,512,512]{2,1,0:T(8,128)(2,1)}, f32[1,512]{1,0:T(1,128)}) custom-call(bf16[2,2,8,512,128]{4,3,2,1,0:T(8,128)(2,1)S(1)} %get-tuple-element.7.turned, bf16[4,4,16,512]{3,2,1,0:T(8,128)(2,1)S(1)} %get-tuple-element.8.feats, bf16[4,4,16,512]{3,2,1,0:T(8,128)(2,1)S(1)} %get-tuple-element.9.gpre), custom_call_target="tpu_custom_call" | custom-call | tf_op jit(solution)/shard_map/dictionary_gradient/pallas_call | solution.py:400
